TPU v7x, 32 devices: a whole 2x2x4 slice. The times are simulated.
32 devices in a mesh: row: 4 (over y, x), col: 8 (over z, core).
Axes of the slice: x: 2, y: 2, z: 4, core: 2. Of those that a mesh axis runs over, the one named last changes fastest.
Arguments:
- gradients: bfloat16 [3, 32, 512, 512], P(None, None, ('row', 'col')), may hold values from -6 to 6
- factors: float32 [2, 32, 512, 512], P(None, None, ('row', 'col')), as said below
- slot_block: int32 [32], replicated, may hold values from 0 to 31, each once
- layer_of_block: int32 [32], replicated, may hold values from 0 to 3
- layer_step_scale: float32 [4], replicated, may hold values from 0.25 to 4
Outputs:
- new_factors: float32 [2, 32, 512, 512], P(None, ('row', 'col'))
- update: bfloat16 [32, 512, 512], P(None, ('row', 'col'))
Inputs may be any that keep to these rules, and one draw needn't show every extreme that they name: Every block factors[i, b] is symmetric positive definite with eigenvalues of 0.25 or more. `slot_block`: each block number stands in exactly one slot; slot j belongs to owner device j in the order of row+col (one slot per device).
All inputs are finite; a program needn't handle non-finite values.
Results may differ from a plain program's by a relative error of at most 0.0069.
Values may be sent and summed in bfloat16 or wider, within the bound.
A program may use at most 64 MiB of HBM per device.

v0:
```python
import functools

import jax
import jax.numpy as jnp
from jax import lax
from jax.experimental import pallas as pl
from jax.experimental.pallas import tpu as pltpu
from jax.sharding import PartitionSpec as P

MESH = pl.DeviceIdType.MESH
SWITCH = 4

ITERS = 6


def inverse_root(matrix):
    unit_matrix = jnp.eye(matrix.shape[0], dtype=jnp.float32)
    frobenius = jnp.sqrt(jnp.sum(matrix * matrix))
    mixer = matrix / frobenius
    approx = unit_matrix * frobenius ** (-0.25)
    for newton_sweep in range(ITERS):
        factor_p = (5.0 * unit_matrix - mixer) * 0.25
        approx = jnp.dot(approx, factor_p, precision=lax.Precision.HIGHEST)
        second_root_factor = jnp.dot(factor_p, factor_p, precision=lax.Precision.HIGHEST)
        mixer = jnp.dot(
            second_root_factor,
            jnp.dot(second_root_factor, mixer, precision=lax.Precision.HIGHEST),
            precision=lax.Precision.HIGHEST,
        )
    return approx


def plain_body(gradients, factors, slot_block, layer_of_block, layer_step_scale):
    count_steps, block_count, row_slab, block_side = gradients.shape
    row_count = lax.axis_size("row")
    col_count = lax.axis_size("col")
    devices_all = row_count * col_count
    per_device = block_count // devices_all
    ordered_grads = jnp.take(gradients, slot_block, axis=1)
    ordered_factors = jnp.take(factors, slot_block, axis=1)
    owned_grads = lax.all_to_all(
        ordered_grads.reshape(count_steps, block_count, 1, row_slab, block_side),
        ("row", "col"),
        split_axis=1,
        concat_axis=2,
        tiled=True,
    )
    owned_factors = lax.all_to_all(
        ordered_factors.reshape(2, block_count, 1, row_slab, block_side),
        ("row", "col"),
        split_axis=1,
        concat_axis=2,
        tiled=True,
    )
    owned_grads = owned_grads.reshape(count_steps, per_device, block_side, block_side)
    owned_factors = owned_factors.reshape(2, per_device, block_side, block_side)
    first_slot = (lax.axis_index("row") * col_count + lax.axis_index("col")) * per_device
    own_slots = first_slot + jnp.arange(per_device, dtype=jnp.int32)
    own_blocks = jnp.take(slot_block, own_slots)
    own_layers = jnp.take(layer_of_block, own_blocks)
    layer_hits = (
        own_layers[:, None] == jnp.arange(layer_step_scale.shape[0], dtype=jnp.int32)[None, :]
    )
    step_multipliers = jnp.sum(jnp.where(layer_hits, layer_step_scale[None, :], 0.0), axis=1)

    def per_slot(block_position):
        gradient = lax.dynamic_index_in_dim(owned_grads, block_position, 1, keepdims=False)
        held = lax.dynamic_index_in_dim(owned_factors, block_position, 1, keepdims=False)
        gram_left = jnp.einsum(
            "sik,sjk->ij", gradient, gradient, preferred_element_type=jnp.float32
        )
        gram_right = jnp.einsum(
            "ski,skj->ij", gradient, gradient, preferred_element_type=jnp.float32
        )
        left_stat = held[0] + gram_left / block_side
        right_stat = held[1] + gram_right / block_side
        root_left_half = inverse_root(left_stat).astype(jnp.bfloat16)
        root_right_half = inverse_root(right_stat).astype(jnp.bfloat16)
        step_multiplier = lax.dynamic_index_in_dim(
            step_multipliers, block_position, 0, keepdims=False
        )
        left_applied = jnp.dot(
            root_left_half, gradient[count_steps - 1], preferred_element_type=jnp.float32
        ).astype(jnp.bfloat16)
        product = jnp.dot(left_applied, root_right_half, preferred_element_type=jnp.float32)
        return (left_stat, right_stat, (step_multiplier * product).astype(jnp.bfloat16))

    lefts, rights, moved = lax.map(per_slot, jnp.arange(per_device, dtype=jnp.int32))
    new_factors = jnp.stack([lefts, rights])
    returned = lax.all_to_all(
        moved.reshape(1, 1, per_device, devices_all, row_slab, block_side),
        ("row", "col"),
        split_axis=3,
        concat_axis=1,
        tiled=True,
    )
    returned = returned.reshape(block_count, row_slab, block_side)
    update = jnp.zeros_like(returned).at[slot_block].set(returned)
    return (new_factors, update)


def dot(a, b, contract=((1,), (0,))):
    return lax.dot_general(
        a.astype(jnp.bfloat16),
        b.astype(jnp.bfloat16),
        (contract, ((), ())),
        preferred_element_type=jnp.float32,
    )


def fused_kernel(
    rows_of,
    cols_of,
    slot_ref,
    inverse_ref,
    layer_ref,
    scale_ref,
    g_ref,
    f_ref,
    nf_ref,
    upd_ref,
    staged_g,
    staged_f,
    staged_x,
    grads,
    facts,
    cross,
    acc,
    turned,
    mixer,
    approx,
    applied,
    moved,
    returned,
    g_send,
    g_recv,
    f_send,
    f_recv,
    u_send,
    u_recv,
):
    steps, blocks, slab, side = g_ref.shape
    half_cols = cols_of // 2
    chunk = slab * half_cols
    half_side = side // 2
    row = lax.axis_index("row")
    col = lax.axis_index("col")
    me = row * cols_of + col
    half = col // half_cols
    place = col % half_cols

    def strip(index):
        return pl.ds(pl.multiple_of(index * slab, slab), slab)

    def same_half(k):
        return (row + k // half_cols) % rows_of, half * half_cols + (place + k % half_cols) % half_cols

    def other_half(k):
        return (
            (row + k // half_cols) % rows_of,
            (1 - half) * half_cols + (place + k % half_cols) % half_cols,
        )

    pairs = rows_of * half_cols

    barrier = pltpu.get_barrier_semaphore()

    def greet(k, carry):
        @pl.when(k > 0)
        def _():
            pl.semaphore_signal(barrier, inc=1, device_id=same_half(k), device_id_type=MESH)

        pl.semaphore_signal(barrier, inc=1, device_id=other_half(k), device_id_type=MESH)
        return carry

    lax.fori_loop(0, pairs, greet, 0)

    def stage_gradients(slot, carry):
        for step in range(steps):
            staged_g[step, strip(slot), :] = g_ref[step, slot_ref[slot]]
        return carry

    lax.fori_loop(0, blocks, stage_gradients, 0)
    pl.semaphore_wait(barrier, blocks - 1)

    def send_gradients(step):
        def ship(peer):
            target = peer[0] * cols_of + peer[1]
            pltpu.make_async_remote_copy(
                src_ref=staged_g.at[step, strip(target), :],
                dst_ref=grads.at[step, strip(me), :],
                send_sem=g_send.at[step],
                recv_sem=g_recv.at[step],
                device_id=peer,
                device_id_type=MESH,
            ).start()

        def one(k, carry):
            ship(other_half(k))

            @pl.when(k > 0)
            def _():
                ship(same_half(k))

            return carry

        lax.fori_loop(0, pairs, one, 0)
        pltpu.make_async_copy(
            staged_g.at[step, strip(me), :], grads.at[step, strip(me), :], g_recv.at[step]
        ).start()

    send_gradients(0)

    def stage_statistics(slot, carry):
        for which in range(2):
            staged_f[which, strip(slot), :] = f_ref[which, slot_ref[slot]].astype(jnp.bfloat16)
        return carry

    lax.fori_loop(0, blocks, stage_statistics, 0)
    natural = lax.broadcasted_iota(jnp.int32, (side, half_side), 0)
    packed = lax.broadcasted_iota(jnp.int32, (side, half_side), 1)
    doubled = 2 * packed - (packed & (chunk - 1))
    pick = jnp.where(natural == doubled + half * chunk, 1.0, 0.0).astype(jnp.bfloat16)
    for which in range(2):
        staged_x[which] = dot(staged_f[which], pick).astype(jnp.bfloat16)

    def send_statistics(k, carry):
        far = other_half(k)
        pltpu.make_async_remote_copy(
            src_ref=staged_x.at[:, strip(far[0] * cols_of + far[1]), :],
            dst_ref=cross.at[:, strip(me), :],
            send_sem=f_send.at[1],
            recv_sem=f_recv.at[1],
            device_id=far,
            device_id_type=MESH,
        ).start()

        @pl.when(k > 0)
        def _():
            near = same_half(k)
            pltpu.make_async_remote_copy(
                src_ref=staged_f.at[:, strip(near[0] * cols_of + near[1]), :],
                dst_ref=facts.at[:, strip(me), :],
                send_sem=f_send.at[0],
                recv_sem=f_recv.at[0],
                device_id=near,
                device_id_type=MESH,
            ).start()

        return carry

    lax.fori_loop(0, pairs, send_statistics, 0)
    pltpu.make_async_copy(
        staged_f.at[:, strip(me), :], facts.at[:, strip(me), :], f_recv.at[0]
    ).start()
    for step in range(1, steps):
        send_gradients(step)

    def wait_gradients(step):
        pltpu.make_async_copy(staged_g.at[step], grads.at[step], g_recv.at[step]).wait()

    def add_gram(step):
        held = grads[step]
        left = dot(held, held, ((1,), (1,)))
        right = dot(held, held, ((0,), (0,)))
        if step == 0:
            acc[0] = left
            acc[1] = right
        else:
            acc[0] += left
            acc[1] += right

    wait_gradients(0)
    add_gram(0)

    pltpu.make_async_copy(
        staged_f.at[:, pl.ds(0, half_side), :], facts.at[:, pl.ds(0, half_side), :], f_recv.at[0]
    ).wait()
    pltpu.make_async_copy(
        staged_x.at[:, pl.ds(0, half_side), :], cross.at[:, pl.ds(0, half_side), :], f_recv.at[1]
    ).wait()
    wide_packed = lax.broadcasted_iota(jnp.int32, (half_side, side), 0)
    wide_natural = lax.broadcasted_iota(jnp.int32, (half_side, side), 1)
    spread = jnp.where(
        wide_natural == 2 * wide_packed - (wide_packed & (chunk - 1)) + (1 - half) * chunk, 1.0, 0.0
    ).astype(jnp.bfloat16)
    lane = lax.broadcasted_iota(jnp.int32, (chunk, side), 1)
    mine = (lane & chunk) == half * chunk
    for which in range(2):
        turned[...] = facts[which].astype(jnp.float32).T
        for part in range(rows_of):
            own = pl.ds(pl.multiple_of(part * 2 * chunk + half * chunk, chunk), chunk)
            rest = pl.ds(pl.multiple_of(part * 2 * chunk + (1 - half) * chunk, chunk), chunk)
            nf_ref[which, 0, own, :] = facts[which, own, :].astype(jnp.float32)
            far = dot(cross[which, rest, :], spread)
            nf_ref[which, 0, rest, :] = jnp.where(mine, turned[rest, :], far)

    for step in range(1, steps):
        wait_gradients(step)
        add_gram(step)

    eye = (
        lax.broadcasted_iota(jnp.int32, (side, side), 0)
        == lax.broadcasted_iota(jnp.int32, (side, side), 1)
    )
    unit = jnp.where(eye, 1.0, 0.0).astype(jnp.float32)
    for which in range(2):
        stat = nf_ref[which, 0] + acc[which] / side
        nf_ref[which, 0] = stat
        total = jnp.sum(jnp.sum(stat * stat, axis=0, keepdims=True), axis=1, keepdims=True)
        frobenius = jnp.sqrt(total)
        start = 1.0 / jnp.sqrt(jnp.sqrt(frobenius))
        mixer[which] = stat / frobenius
        approx[which] = start * (1.25 * unit - 0.25 * mixer[which])

    def grow(which):
        m = mixer[which]
        lead = (dot(m, m) - 10.0 * m) * 0.0625
        inner = 1.5625 * m + dot(lead, m)
        return 1.5625 * inner + dot(lead, inner)

    for sweep in range(SWITCH):
        for which in range(2):
            if sweep > 0:
                x = approx[which]
                approx[which] = 1.25 * x - 0.25 * dot(x, mixer[which])
            grown = grow(which)
            mixer[which] = grown - unit if sweep == SWITCH - 1 else grown
    for sweep in range(SWITCH, ITERS):
        for which in range(2):
            x, e = approx[which], mixer[which]
            approx[which] = x - 0.25 * dot(x, e)
            if sweep < ITERS - 1:
                lead = 0.0625 * dot(e, e) - 0.5 * e
                inner = lead + e + dot(lead, e)
                mixer[which] = lead + inner + dot(lead, inner)

    multiplier = scale_ref[layer_ref[slot_ref[me]]]
    applied[...] = dot(approx[0], grads[steps - 1]).astype(jnp.bfloat16)
    right_half = approx[1].astype(jnp.bfloat16)
    band = slab * cols_of
    for turn in range(rows_of):
        target_row = (row + turn) % rows_of
        rows = pl.ds(pl.multiple_of(target_row * band, band), band)
        moved[rows, :] = (multiplier * dot(applied[rows, :], right_half)).astype(jnp.bfloat16)

        def give_back(k, carry):
            target_col = (col + 3 * k) % cols_of
            target = target_row * cols_of + target_col
            pltpu.make_async_remote_copy(
                src_ref=moved.at[strip(target), :],
                dst_ref=returned.at[me],
                send_sem=u_send,
                recv_sem=u_recv,
                device_id=(target_row, target_col),
                device_id_type=MESH,
            ).start()
            return carry

        lax.fori_loop(1 if turn == 0 else 0, cols_of, give_back, 0)
    pltpu.make_async_copy(moved.at[strip(me), :], returned.at[me], u_recv).start()

    most = side - slab
    for step in range(steps):
        sent = staged_g.at[step, pl.ds(0, most), :]
        pltpu.make_async_copy(sent, sent, g_send.at[step]).wait()
    near = staged_f.at[:, pl.ds(0, half_side - slab), :]
    pltpu.make_async_copy(near, near, f_send.at[0]).wait()
    far = staged_x.at[:, pl.ds(0, half_side), :]
    pltpu.make_async_copy(far, far, f_send.at[1]).wait()
    pltpu.make_async_copy(returned, returned, u_recv).wait()

    def unpack(block, carry):
        upd_ref[block] = returned[inverse_ref[block]]
        return carry

    lax.fori_loop(0, blocks, unpack, 0)
    pltpu.make_async_copy(
        moved.at[pl.ds(0, most), :], moved.at[pl.ds(0, most), :], u_send
    ).wait()


def fused_body(rows_of, cols_of, gradients, factors, slot_block, layer_of_block, layer_step_scale):
    steps, blocks, slab, side = gradients.shape
    half_side = side // 2
    in_vmem = pl.BlockSpec(memory_space=pltpu.VMEM)
    in_smem = pl.BlockSpec(memory_space=pltpu.SMEM)
    bf16, f32 = jnp.bfloat16, jnp.float32
    order = jnp.arange(blocks, dtype=jnp.int32)
    inverse = jnp.sum(jnp.where(slot_block[None, :] == order[:, None], order[None, :], 0), axis=1)
    return pl.pallas_call(
        functools.partial(fused_kernel, rows_of, cols_of),
        out_shape=(
            jax.ShapeDtypeStruct((2, 1, side, side), f32),
            jax.ShapeDtypeStruct((blocks, slab, side), bf16),
        ),
        in_specs=[in_smem] * 4 + [in_vmem] * 2,
        out_specs=(in_vmem, in_vmem),
        scratch_shapes=[
            pltpu.VMEM((steps, side, side), bf16),
            pltpu.VMEM((2, side, side), bf16),
            pltpu.VMEM((2, side, half_side), bf16),
            pltpu.VMEM((steps, side, side), bf16),
            pltpu.VMEM((2, side, side), bf16),
            pltpu.VMEM((2, side, half_side), bf16),
            pltpu.VMEM((2, side, side), f32),
            pltpu.VMEM((side, side), f32),
            pltpu.VMEM((2, side, side), f32),
            pltpu.VMEM((2, side, side), f32),
            pltpu.VMEM((side, side), bf16),
            pltpu.VMEM((side, side), bf16),
            pltpu.VMEM((blocks, slab, side), bf16),
            pltpu.SemaphoreType.DMA((steps,)),
            pltpu.SemaphoreType.DMA((steps,)),
            pltpu.SemaphoreType.DMA((2,)),
            pltpu.SemaphoreType.DMA((2,)),
            pltpu.SemaphoreType.DMA,
            pltpu.SemaphoreType.DMA,
        ],
        compiler_params=pltpu.CompilerParams(
            collective_id=0, has_side_effects=True, vmem_limit_bytes=56 * 1024 * 1024
        ),
    )(slot_block, inverse, layer_of_block, layer_step_scale, gradients, factors)


def fits(rows_of, cols_of, blocks, slab, side):
    chunk = slab * cols_of // 2
    return (
        blocks == rows_of * cols_of
        and slab % 16 == 0
        and cols_of % 2 == 0
        and cols_of % 3 != 0
        and chunk & (chunk - 1) == 0
        and side % 256 == 0
    )


def solution(mesh):
    rows_of, cols_of = mesh.shape["row"], mesh.shape["col"]

    def body(gradients, factors, *rest):
        _, blocks, slab, side = gradients.shape
        if fits(rows_of, cols_of, blocks, slab, side):
            return fused_body(rows_of, cols_of, gradients, factors, *rest)
        return plain_body(gradients, factors, *rest)

    return jax.shard_map(
        body,
        mesh=mesh,
        in_specs=(
            P(None, None, ("row", "col"), None),
            P(None, None, ("row", "col"), None),
            P(),
            P(),
            P(),
        ),
        out_specs=(P(None, ("row", "col"), None, None), P(None, ("row", "col"), None)),
        check_vma=False,
    )
```

profile of v0, /device:TPU:0, one launch (start us, length us, event | category | flops | bytes accessed | tf_op | source)
XLA Modules:
  0.0 91.8 jit_solution(2709598398962615203)
XLA Ops:
  0.6 1.3 %select_reduce_fusion.inverse_ref = s32[32]{0:T(128)} fusion(s32[32]{0:T(128)} %slot_ref.1), kind=kLoop, calls=%fused_computation | loop fusion | flops 3040 | bytes 256 | tf_op jit(solution)/shard_map/reduce_sum | solution.py:390
  1.9 85.9 %shard_map.68 = (f32[2,1,512,512]{3,2,1,0:T(8,128)}, bf16[32,16,512]{2,1,0:T(8,128)(2,1)}) custom-call(s32[32]{0:T(128)} %slot_ref.1, s32[32]{0:T(128)} %select_reduce_fusion.inverse_ref, s32[32]{0:T(128)} %layer_ref.1, f32[4]{0:T(128)} %scale_ref.1, bf16[3,32,16,512]{3,2,1,0:T(8,128)(2,1)} %g_ref.1, f32[2,32,16,512]{3,2,1,0:T(8,128)} %f_ref.1), custom_call_target="tpu_custom_call" | custom-call | tf_op jit(solution)/shard_map/pallas_call | solution.py:391
  87.8 0.0 copy-start
  87.8 3.1 %copy.9 = f32[2,1,512,512]{3,2,1,0:T(8,128)} copy(f32[2,1,512,512]{3,2,1,0:T(8,128)} %get-tuple-element.4) | data formatting | bytes 4194304
  91.0 0.0 copy-done
  91.0 0.8 copy.10
Async XLA Ops:
  87.8 3.1 %copy-start = (bf16[32,16,512]{2,1,0:T(8,128)(2,1)S(1)}, bf16[32,16,512]{2,1,0:T(8,128)(2,1)}, u32[]{:S(2)}) copy-start(bf16[32,16,512]{2,1,0:T(8,128)(2,1)} %get-tuple-element.5) | copy-start | bytes 1572868
where the time goes:
time: 91.9 us; the launch traced here: 91.8 us
  Pallas kernels  85.9 us (93%)
  local copies, waits for them, and re-layouts  3.93 us (4%)
  other arithmetic  1.28 us (1%)
    pallas_call x1, Pallas kernels, fused_body(): pl.pallas_call(functools.partial(fused_kernel, rows_of, cols_of), out_sha...  85.9 us
    unnamed x4, local copies, waits for them, and re-layouts  3.93 us

commit v1 on v0

--- a/solution.py
+++ b/solution.py
@@ -115,10 +115,12 @@
     inverse_ref,
     layer_ref,
     scale_ref,
+    g_far,
+    f_far,
+    nf_ref,
+    upd_ref,
     g_ref,
     f_ref,
-    nf_ref,
-    upd_ref,
     staged_g,
     staged_f,
     staged_x,
@@ -138,6 +140,7 @@
     f_recv,
     u_send,
     u_recv,
+    in_sem,
 ):
     steps, blocks, slab, side = g_ref.shape
     half_cols = cols_of // 2
@@ -162,6 +165,10 @@
         )
 
     pairs = rows_of * half_cols
+    g_fetch = pltpu.make_async_copy(g_far, g_ref, in_sem.at[0])
+    f_fetch = pltpu.make_async_copy(f_far, f_ref, in_sem.at[1])
+    g_fetch.start()
+    f_fetch.start()
 
     barrier = pltpu.get_barrier_semaphore()
 
@@ -175,12 +182,15 @@
 
     lax.fori_loop(0, pairs, greet, 0)
 
-    def stage_gradients(slot, carry):
-        for step in range(steps):
+    def stage_gradients(step):
+        def one(slot, carry):
             staged_g[step, strip(slot), :] = g_ref[step, slot_ref[slot]]
-        return carry
-
-    lax.fori_loop(0, blocks, stage_gradients, 0)
+            return carry
+
+        lax.fori_loop(0, blocks, one, 0, unroll=4)
+
+    g_fetch.wait()
+    stage_gradients(0)
     pl.semaphore_wait(barrier, blocks - 1)
 
     def send_gradients(step):
@@ -216,7 +226,8 @@
             staged_f[which, strip(slot), :] = f_ref[which, slot_ref[slot]].astype(jnp.bfloat16)
         return carry
 
-    lax.fori_loop(0, blocks, stage_statistics, 0)
+    f_fetch.wait()
+    lax.fori_loop(0, blocks, stage_statistics, 0, unroll=2)
     natural = lax.broadcasted_iota(jnp.int32, (side, half_side), 0)
     packed = lax.broadcasted_iota(jnp.int32, (side, half_side), 1)
     doubled = 2 * packed - (packed & (chunk - 1))
@@ -254,6 +265,7 @@
         staged_f.at[:, strip(me), :], facts.at[:, strip(me), :], f_recv.at[0]
     ).start()
     for step in range(1, steps):
+        stage_gradients(step)
         send_gradients(step)
 
     def wait_gradients(step):
@@ -313,27 +325,35 @@
         mixer[which] = stat / frobenius
         approx[which] = start * (1.25 * unit - 0.25 * mixer[which])
 
-    def grow(which):
-        m = mixer[which]
-        lead = (dot(m, m) - 10.0 * m) * 0.0625
-        inner = 1.5625 * m + dot(lead, m)
-        return 1.5625 * inner + dot(lead, inner)
+    def both(left, right):
+        return [dot(a, b) for a, b in zip(left, right)]
 
     for sweep in range(SWITCH):
-        for which in range(2):
-            if sweep > 0:
-                x = approx[which]
-                approx[which] = 1.25 * x - 0.25 * dot(x, mixer[which])
-            grown = grow(which)
+        m = [mixer[0], mixer[1]]
+        square = both(m, m)
+        if sweep > 0:
+            x = [approx[0], approx[1]]
+            step_x = both(x, m)
+            for which in range(2):
+                approx[which] = 1.25 * x[which] - 0.25 * step_x[which]
+        lead = [0.0625 * square[which] - 0.625 * m[which] for which in range(2)]
+        inner = [1.5625 * m[which] + part for which, part in enumerate(both(lead, m))]
+        for which, part in enumerate(both(lead, inner)):
+            grown = 1.5625 * inner[which] + part
             mixer[which] = grown - unit if sweep == SWITCH - 1 else grown
     for sweep in range(SWITCH, ITERS):
+        e = [mixer[0], mixer[1]]
+        if sweep < ITERS - 1:
+            square = both(e, e)
+        x = [approx[0], approx[1]]
+        step_x = both(x, e)
         for which in range(2):
-            x, e = approx[which], mixer[which]
-            approx[which] = x - 0.25 * dot(x, e)
-            if sweep < ITERS - 1:
-                lead = 0.0625 * dot(e, e) - 0.5 * e
-                inner = lead + e + dot(lead, e)
-                mixer[which] = lead + inner + dot(lead, inner)
+            approx[which] = x[which] - 0.25 * step_x[which]
+        if sweep < ITERS - 1:
+            lead = [0.0625 * square[which] - 0.5 * e[which] for which in range(2)]
+            inner = [lead[which] + e[which] + part for which, part in enumerate(both(lead, e))]
+            for which, part in enumerate(both(lead, inner)):
+                mixer[which] = lead[which] + inner[which] + part
 
     multiplier = scale_ref[layer_ref[slot_ref[me]]]
     applied[...] = dot(approx[0], grads[steps - 1]).astype(jnp.bfloat16)
@@ -391,12 +411,14 @@
     return pl.pallas_call(
         functools.partial(fused_kernel, rows_of, cols_of),
         out_shape=(
-            jax.ShapeDtypeStruct((2, 1, side, side), f32),
-            jax.ShapeDtypeStruct((blocks, slab, side), bf16),
+            pltpu.VMEM((2, 1, side, side), f32),
+            pltpu.VMEM((blocks, slab, side), bf16),
         ),
-        in_specs=[in_smem] * 4 + [in_vmem] * 2,
+        in_specs=[in_smem] * 4 + [pl.BlockSpec(memory_space=pl.ANY)] * 2,
         out_specs=(in_vmem, in_vmem),
         scratch_shapes=[
+            pltpu.VMEM(gradients.shape, bf16),
+            pltpu.VMEM(factors.shape, f32),
             pltpu.VMEM((steps, side, side), bf16),
             pltpu.VMEM((2, side, side), bf16),
             pltpu.VMEM((2, side, half_side), bf16),
@@ -416,6 +438,7 @@
             pltpu.SemaphoreType.DMA((2,)),
             pltpu.SemaphoreType.DMA,
             pltpu.SemaphoreType.DMA,
+            pltpu.SemaphoreType.DMA((2,)),
         ],
         compiler_params=pltpu.CompilerParams(
             collective_id=0, has_side_effects=True, vmem_limit_bytes=56 * 1024 * 1024

time: 91.9 us -> 87 us (0.947)
  Pallas kernels: 85.9 us -> 82.8 us
  local copies, waits for them, and re-layouts: 3.93 us -> 2.11 us
    pallas_call x1, Pallas kernels: 85.9 us -> 82.8 us  [fused_body(): pl.pallas_call(functools.partial(fused_kernel, rows_of, cols_of), out_sha...]
    unnamed x4 -> x2, local copies, waits for them, and re-layouts: 3.93 us -> 2.11 us
where the time goes in v1:
time: 87 us; the launch traced here: 86.8 us
  Pallas kernels  82.8 us (95%)
  local copies, waits for them, and re-layouts  2.11 us (2%)
  other arithmetic  1.28 us (1%)
    pallas_call x1, Pallas kernels, fused_body(): pl.pallas_call(functools.partial(fused_kernel, rows_of, cols_of), out_sha...  82.8 us
    unnamed x2, local copies, waits for them, and re-layouts  2.11 us

profile of v1, /device:TPU:0, one launch (start us, length us, event | category | flops | bytes accessed | tf_op | source)
XLA Modules:
  0.0 86.8 jit_solution(13385678093142912930)
XLA Ops:
  0.6 1.3 %select_reduce_fusion.inverse_ref = s32[32]{0:T(128)} fusion(s32[32]{0:T(128)} %slot_ref.1), kind=kLoop, calls=%fused_computation | loop fusion | flops 3040 | bytes 256 | tf_op jit(solution)/shard_map/reduce_sum | solution.py:410
  1.9 82.8 %shard_map.68 = (f32[2,1,512,512]{3,2,1,0:T(8,128)S(1)}, bf16[32,16,512]{2,1,0:T(8,128)(2,1)S(1)}) custom-call(s32[32]{0:T(128)} %slot_ref.1, s32[32]{0:T(128)} %select_reduce_fusion.inverse_ref, s32[32]{0:T(128)} %layer_ref.1, f32[4]{0:T(128)} %scale_ref.1, bf16[3,32,16,512]{3,2,1,0:T(8,128)(2,1)} %g_far.1, f32[2,32,16,512]{3,2,1,0:T(8,128)} %f_far.1), custom_call_target="tpu_custom_call" | custom-call | tf_op jit(solution)/shard_map/pallas_call | solution.py:411
  84.7 1.3 %copy.9 = f32[2,1,512,512]{3,2,1,0:T(8,128)} copy(f32[2,1,512,512]{3,2,1,0:T(8,128)S(1)} %get-tuple-element.2) | data formatting | bytes 4194304
  86.0 0.8 copy.10

commit v2 on v1

--- a/solution.py
+++ b/solution.py
@@ -8,9 +8,8 @@
 from jax.sharding import PartitionSpec as P
 
 MESH = pl.DeviceIdType.MESH
-SWITCH = 4
-
 ITERS = 6
+SWITCH = ITERS - 2
 
 
 def inverse_root(matrix):
@@ -112,7 +111,6 @@
     rows_of,
     cols_of,
     slot_ref,
-    inverse_ref,
     layer_ref,
     scale_ref,
     g_far,
@@ -141,6 +139,7 @@
     u_send,
     u_recv,
     in_sem,
+    inverse_ref,
 ):
     steps, blocks, slab, side = g_ref.shape
     half_cols = cols_of // 2
@@ -228,12 +227,21 @@
 
     f_fetch.wait()
     lax.fori_loop(0, blocks, stage_statistics, 0, unroll=2)
-    natural = lax.broadcasted_iota(jnp.int32, (side, half_side), 0)
-    packed = lax.broadcasted_iota(jnp.int32, (side, half_side), 1)
-    doubled = 2 * packed - (packed & (chunk - 1))
-    pick = jnp.where(natural == doubled + half * chunk, 1.0, 0.0).astype(jnp.bfloat16)
+    natural = lax.broadcasted_iota(jnp.int32, (side, 2 * chunk), 0)
+    packed = lax.broadcasted_iota(jnp.int32, (side, 2 * chunk), 1)
+    low = packed < chunk
+    within = packed & (chunk - 1)
+    bands = [((row + ahead) % rows_of) * 2 * chunk + half * chunk for ahead in range(3)]
+
+    def pick(first, second):
+        hit = natural == within + jnp.where(low, first, second)
+        return jnp.where(hit, 1.0, 0.0).astype(jnp.bfloat16)
+
     for which in range(2):
-        staged_x[which] = dot(staged_f[which], pick).astype(jnp.bfloat16)
+        staged_x[which] = dot(staged_f[which], pick(bands[0], bands[1])).astype(jnp.bfloat16)
+    staged_x[2] = (
+        dot(staged_f[0], pick(bands[2], -side)) + dot(staged_f[1], pick(-side, bands[2]))
+    ).astype(jnp.bfloat16)
 
     def send_statistics(k, carry):
         far = other_half(k)
@@ -268,6 +276,15 @@
         stage_gradients(step)
         send_gradients(step)
 
+    def find(block, carry):
+        found = jnp.int32(0)
+        for slot in range(blocks):
+            found = found + (slot - found) * (slot_ref[slot] == block).astype(jnp.int32)
+        inverse_ref[block] = found
+        return carry
+
+    lax.fori_loop(0, blocks, find, 0)
+
     def wait_gradients(step):
         pltpu.make_async_copy(staged_g.at[step], grads.at[step], g_recv.at[step]).wait()
 
@@ -291,21 +308,39 @@
     pltpu.make_async_copy(
         staged_x.at[:, pl.ds(0, half_side), :], cross.at[:, pl.ds(0, half_side), :], f_recv.at[1]
     ).wait()
-    wide_packed = lax.broadcasted_iota(jnp.int32, (half_side, side), 0)
-    wide_natural = lax.broadcasted_iota(jnp.int32, (half_side, side), 1)
-    spread = jnp.where(
-        wide_natural == 2 * wide_packed - (wide_packed & (chunk - 1)) + (1 - half) * chunk, 1.0, 0.0
-    ).astype(jnp.bfloat16)
+    wide_packed = lax.broadcasted_iota(jnp.int32, (2 * chunk, side), 0)
+    wide_natural = lax.broadcasted_iota(jnp.int32, (2 * chunk, side), 1)
+    wide_low = wide_packed < chunk
+    wide_within = wide_packed & (chunk - 1)
+
+    def spread(first, second):
+        hit = wide_natural == wide_within + jnp.where(wide_low, first, second)
+        return jnp.where(hit, 1.0, 0.0).astype(jnp.bfloat16)
+
+    def far_band(part):
+        return (part % rows_of) * 2 * chunk + (1 - half) * chunk
+
     lane = lax.broadcasted_iota(jnp.int32, (chunk, side), 1)
-    mine = (lane & chunk) == half * chunk
+    for part in range(rows_of):
+        rest = pl.ds(pl.multiple_of(far_band(part), chunk), chunk)
+        wide = spread(far_band(part), far_band(part + 1))
+        extras = (spread(far_band(part + 2), -side), spread(-side, far_band(part + 2)))
+        for which in range(2):
+            facts[which, rest, :] = (
+                dot(cross[which, rest, :], wide) + dot(cross[2, rest, :], extras[which])
+            ).astype(jnp.bfloat16)
     for which in range(2):
         turned[...] = facts[which].astype(jnp.float32).T
         for part in range(rows_of):
             own = pl.ds(pl.multiple_of(part * 2 * chunk + half * chunk, chunk), chunk)
-            rest = pl.ds(pl.multiple_of(part * 2 * chunk + (1 - half) * chunk, chunk), chunk)
+            rest = pl.ds(pl.multiple_of(far_band(part), chunk), chunk)
+            mirrored = ((lane & chunk) == half * chunk) | (
+                (lane & (side - chunk)) == far_band(part + 3)
+            )
             nf_ref[which, 0, own, :] = facts[which, own, :].astype(jnp.float32)
-            far = dot(cross[which, rest, :], spread)
-            nf_ref[which, 0, rest, :] = jnp.where(mine, turned[rest, :], far)
+            nf_ref[which, 0, rest, :] = jnp.where(
+                mirrored, turned[rest, :], facts[which, rest, :].astype(jnp.float32)
+            )
 
     for step in range(1, steps):
         wait_gradients(step)
@@ -341,19 +376,22 @@
         for which, part in enumerate(both(lead, inner)):
             grown = 1.5625 * inner[which] + part
             mixer[which] = grown - unit if sweep == SWITCH - 1 else grown
-    for sweep in range(SWITCH, ITERS):
-        e = [mixer[0], mixer[1]]
-        if sweep < ITERS - 1:
-            square = both(e, e)
-        x = [approx[0], approx[1]]
-        step_x = both(x, e)
-        for which in range(2):
-            approx[which] = x[which] - 0.25 * step_x[which]
-        if sweep < ITERS - 1:
-            lead = [0.0625 * square[which] - 0.5 * e[which] for which in range(2)]
-            inner = [lead[which] + e[which] + part for which, part in enumerate(both(lead, e))]
-            for which, part in enumerate(both(lead, inner)):
-                mixer[which] = lead[which] + inner[which] + part
+    e = [mixer[0], mixer[1]]
+    x = [approx[0], approx[1]]
+    square = both(e, e)
+    cube = both(square, e)
+    high = [
+        0.0341796875 * e[which]
+        - 0.004638671875 * square[which]
+        + 0.000244140625 * cube[which]
+        for which in range(2)
+    ]
+    shift = [
+        0.15625 * square[which] - 0.25 * e[which] - 0.1171875 * cube[which] + part
+        for which, part in enumerate(both(cube, high))
+    ]
+    for which, part in enumerate(both(x, shift)):
+        approx[which] = x[which] + part
 
     multiplier = scale_ref[layer_ref[slot_ref[me]]]
     applied[...] = dot(approx[0], grads[steps - 1]).astype(jnp.bfloat16)
@@ -402,29 +440,26 @@
 
 def fused_body(rows_of, cols_of, gradients, factors, slot_block, layer_of_block, layer_step_scale):
     steps, blocks, slab, side = gradients.shape
-    half_side = side // 2
     in_vmem = pl.BlockSpec(memory_space=pltpu.VMEM)
     in_smem = pl.BlockSpec(memory_space=pltpu.SMEM)
     bf16, f32 = jnp.bfloat16, jnp.float32
-    order = jnp.arange(blocks, dtype=jnp.int32)
-    inverse = jnp.sum(jnp.where(slot_block[None, :] == order[:, None], order[None, :], 0), axis=1)
     return pl.pallas_call(
         functools.partial(fused_kernel, rows_of, cols_of),
         out_shape=(
             pltpu.VMEM((2, 1, side, side), f32),
             pltpu.VMEM((blocks, slab, side), bf16),
         ),
-        in_specs=[in_smem] * 4 + [pl.BlockSpec(memory_space=pl.ANY)] * 2,
+        in_specs=[in_smem] * 3 + [pl.BlockSpec(memory_space=pl.ANY)] * 2,
         out_specs=(in_vmem, in_vmem),
         scratch_shapes=[
             pltpu.VMEM(gradients.shape, bf16),
             pltpu.VMEM(factors.shape, f32),
             pltpu.VMEM((steps, side, side), bf16),
             pltpu.VMEM((2, side, side), bf16),
-            pltpu.VMEM((2, side, half_side), bf16),
+            pltpu.VMEM((3, side, 2 * slab * cols_of // 2), bf16),
             pltpu.VMEM((steps, side, side), bf16),
             pltpu.VMEM((2, side, side), bf16),
-            pltpu.VMEM((2, side, half_side), bf16),
+            pltpu.VMEM((3, side, 2 * slab * cols_of // 2), bf16),
             pltpu.VMEM((2, side, side), f32),
             pltpu.VMEM((side, side), f32),
             pltpu.VMEM((2, side, side), f32),
@@ -439,17 +474,21 @@
             pltpu.SemaphoreType.DMA,
             pltpu.SemaphoreType.DMA,
             pltpu.SemaphoreType.DMA((2,)),
+            pltpu.SMEM((blocks,), jnp.int32),
         ],
         compiler_params=pltpu.CompilerParams(
             collective_id=0, has_side_effects=True, vmem_limit_bytes=56 * 1024 * 1024
         ),
-    )(slot_block, inverse, layer_of_block, layer_step_scale, gradients, factors)
+    )(slot_block, layer_of_block, layer_step_scale, gradients, factors)
 
 
 def fits(rows_of, cols_of, blocks, slab, side):
     chunk = slab * cols_of // 2
     return (
         blocks == rows_of * cols_of
+        and rows_of == 4
+        and 2 * chunk == 128
+        and side & (side - 1) == 0
         and slab % 16 == 0
         and cols_of % 2 == 0
         and cols_of % 3 != 0

time: 87 us -> 82.6 us (0.949)
  Pallas kernels: 82.8 us -> 79.6 us
  other arithmetic: 1.28 us -> 0 us
    pallas_call x1, Pallas kernels: 82.8 us -> 79.6 us  [fused_body(): pl.pallas_call(functools.partial(fused_kernel, rows_of, cols_of), out_sha...]
    reduce_sum x1 -> x0, other arithmetic: 1.28 us -> none  [fused_body(): jnp.sum(jnp.where(slot_block[None, :] == order[:, None], order[None, :],...]
where the time goes in v2:
time: 82.6 us; the launch traced here: 82.4 us
  Pallas kernels  79.6 us (96%)
  local copies, waits for them, and re-layouts  2.11 us (3%)
    pallas_call x1, Pallas kernels, fused_body(): pl.pallas_call(functools.partial(fused_kernel, rows_of, cols_of), out_sha...  79.6 us
    unnamed x2, local copies, waits for them, and re-layouts  2.11 us

profile of v2, /device:TPU:0, one launch (start us, length us, event | category | flops | bytes accessed | tf_op | source)
XLA Modules:
  0.0 82.4 jit_solution(7227402425006964334)
XLA Ops:
  0.6 79.6 %shard_map.68 = (f32[2,1,512,512]{3,2,1,0:T(8,128)S(1)}, bf16[32,16,512]{2,1,0:T(8,128)(2,1)S(1)}) custom-call(s32[32]{0:T(128)} %slot_ref.1, s32[32]{0:T(128)} %layer_ref.1, f32[4]{0:T(128)} %scale_ref.1, bf16[3,32,16,512]{3,2,1,0:T(8,128)(2,1)} %g_far.1, f32[2,32,16,512]{3,2,1,0:T(8,128)} %f_far.1), custom_call_target="tpu_custom_call" | custom-call | tf_op jit(solution)/shard_map/pallas_call | solution.py:446
  80.3 1.3 %copy.9 = f32[2,1,512,512]{3,2,1,0:T(8,128)} copy(f32[2,1,512,512]{3,2,1,0:T(8,128)S(1)} %get-tuple-element.2) | data formatting | bytes 4194304
  81.6 0.8 copy.10

commit v3 on v2

--- a/solution.py
+++ b/solution.py
@@ -127,8 +127,6 @@
     cross,
     acc,
     turned,
-    mixer,
-    approx,
     applied,
     moved,
     returned,
@@ -346,56 +344,89 @@
         wait_gradients(step)
         add_gram(step)
 
-    eye = (
-        lax.broadcasted_iota(jnp.int32, (side, side), 0)
-        == lax.broadcasted_iota(jnp.int32, (side, side), 1)
-    )
-    unit = jnp.where(eye, 1.0, 0.0).astype(jnp.float32)
-    for which in range(2):
+    hs = side // 2
+
+    def unit_of(shape):
+        hit = lax.broadcasted_iota(jnp.int32, shape, 0) == lax.broadcasted_iota(jnp.int32, shape, 1)
+        return jnp.where(hit, 1.0, 0.0).astype(jnp.float32)
+
+    unit = (unit_of((hs, side)), unit_of((hs, hs)))
+
+    def per_part(form, *matrices):
+        return tuple(form(*parts) for parts in zip(*matrices))
+
+    def operand(matrix):
+        upper, corner = matrix
+        lower = jnp.concatenate([upper[:, hs:].T, corner], axis=1)
+        return jnp.concatenate([upper.astype(jnp.bfloat16), lower.astype(jnp.bfloat16)], axis=0)
+
+    def operands(matrices):
+        return [operand(matrix) for matrix in matrices]
+
+    def both(left, right):
+        return [(dot(p[:hs], q), dot(p[hs:], q[:, hs:])) for p, q in zip(left, right)]
+
+    sides = range(2)
+    m, x = [], []
+    for which in sides:
         stat = nf_ref[which, 0] + acc[which] / side
         nf_ref[which, 0] = stat
         total = jnp.sum(jnp.sum(stat * stat, axis=0, keepdims=True), axis=1, keepdims=True)
         frobenius = jnp.sqrt(total)
         start = 1.0 / jnp.sqrt(jnp.sqrt(frobenius))
-        mixer[which] = stat / frobenius
-        approx[which] = start * (1.25 * unit - 0.25 * mixer[which])
-
-    def both(left, right):
-        return [dot(a, b) for a, b in zip(left, right)]
+        scaled = (stat[:hs] / frobenius, stat[hs:, hs:] / frobenius)
+        m.append(scaled)
+        x.append(per_part(lambda u, v: start * (1.25 * u - 0.25 * v), unit, scaled))
 
     for sweep in range(SWITCH):
-        m = [mixer[0], mixer[1]]
-        square = both(m, m)
+        m_op = operands(m)
+        square = both(m_op, m_op)
         if sweep > 0:
-            x = [approx[0], approx[1]]
-            step_x = both(x, m)
-            for which in range(2):
-                approx[which] = 1.25 * x[which] - 0.25 * step_x[which]
-        lead = [0.0625 * square[which] - 0.625 * m[which] for which in range(2)]
-        inner = [1.5625 * m[which] + part for which, part in enumerate(both(lead, m))]
-        for which, part in enumerate(both(lead, inner)):
-            grown = 1.5625 * inner[which] + part
-            mixer[which] = grown - unit if sweep == SWITCH - 1 else grown
-    e = [mixer[0], mixer[1]]
-    x = [approx[0], approx[1]]
-    square = both(e, e)
-    cube = both(square, e)
-    high = [
-        0.0341796875 * e[which]
-        - 0.004638671875 * square[which]
-        + 0.000244140625 * cube[which]
-        for which in range(2)
-    ]
-    shift = [
-        0.15625 * square[which] - 0.25 * e[which] - 0.1171875 * cube[which] + part
-        for which, part in enumerate(both(cube, high))
-    ]
-    for which, part in enumerate(both(x, shift)):
-        approx[which] = x[which] + part
+            step_x = both(operands(x), m_op)
+            x = [per_part(lambda u, v: 1.25 * u - 0.25 * v, x[w], step_x[w]) for w in sides]
+        lead = operands(
+            [per_part(lambda u, v: 0.0625 * u - 0.625 * v, square[w], m[w]) for w in sides]
+        )
+        product = both(lead, m_op)
+        inner = [per_part(lambda u, v: 1.5625 * u + v, m[w], product[w]) for w in sides]
+        product = both(lead, operands(inner))
+        m = [per_part(lambda u, v: 1.5625 * u + v, inner[w], product[w]) for w in sides]
+
+    e = [per_part(lambda u, v: u - v, m[w], unit) for w in sides]
+    e_op = operands(e)
+    square = both(e_op, e_op)
+    cube = both(operands(square), e_op)
+    high = operands(
+        [
+            per_part(
+                lambda u, v, w: 0.0341796875 * u - 0.004638671875 * v + 0.000244140625 * w,
+                e[w],
+                square[w],
+                cube[w],
+            )
+            for w in sides
+        ]
+    )
+    product = both(operands(cube), high)
+    shift = operands(
+        [
+            per_part(
+                lambda u, v, w, t: 0.15625 * v - 0.25 * u - 0.1171875 * w + t,
+                e[w],
+                square[w],
+                cube[w],
+                product[w],
+            )
+            for w in sides
+        ]
+    )
+    product = both(operands(x), shift)
+    left_half, right_half = operands(
+        [per_part(lambda u, v: u + v, x[w], product[w]) for w in sides]
+    )
 
     multiplier = scale_ref[layer_ref[slot_ref[me]]]
-    applied[...] = dot(approx[0], grads[steps - 1]).astype(jnp.bfloat16)
-    right_half = approx[1].astype(jnp.bfloat16)
+    applied[...] = dot(left_half, grads[steps - 1]).astype(jnp.bfloat16)
     band = slab * cols_of
     for turn in range(rows_of):
         target_row = (row + turn) % rows_of
@@ -462,8 +493,6 @@
             pltpu.VMEM((3, side, 2 * slab * cols_of // 2), bf16),
             pltpu.VMEM((2, side, side), f32),
             pltpu.VMEM((side, side), f32),
-            pltpu.VMEM((2, side, side), f32),
-            pltpu.VMEM((2, side, side), f32),
             pltpu.VMEM((side, side), bf16),
             pltpu.VMEM((side, side), bf16),
             pltpu.VMEM((blocks, slab, side), bf16),

time: 82.6 us -> 79.8 us (0.966)
  Pallas kernels: 79.6 us -> 76.8 us
    pallas_call x1, Pallas kernels: 79.6 us -> 76.8 us  [fused_body(): pl.pallas_call(functools.partial(fused_kernel, rows_of, cols_of), out_sha...]
where the time goes in v3:
time: 79.8 us; the launch traced here: 79.6 us
  Pallas kernels  76.8 us (96%)
  local copies, waits for them, and re-layouts  2.11 us (3%)
    pallas_call x1, Pallas kernels, fused_body(): pl.pallas_call(functools.partial(fused_kernel, rows_of, cols_of), out_sha...  76.8 us
    unnamed x2, local copies, waits for them, and re-layouts  2.11 us

profile of v3, /device:TPU:0, one launch (start us, length us, event | category | flops | bytes accessed | tf_op | source)
XLA Modules:
  0.0 79.6 jit_solution(10138196318359584690)
XLA Ops:
  0.6 76.8 %shard_map.68 = (f32[2,1,512,512]{3,2,1,0:T(8,128)S(1)}, bf16[32,16,512]{2,1,0:T(8,128)(2,1)S(1)}) custom-call(s32[32]{0:T(128)} %slot_ref.1, s32[32]{0:T(128)} %layer_ref.1, f32[4]{0:T(128)} %scale_ref.1, bf16[3,32,16,512]{3,2,1,0:T(8,128)(2,1)} %g_far.1, f32[2,32,16,512]{3,2,1,0:T(8,128)} %f_far.1), custom_call_target="tpu_custom_call" | custom-call | tf_op jit(solution)/shard_map/pallas_call | solution.py:477
  77.5 1.3 %copy.9 = f32[2,1,512,512]{3,2,1,0:T(8,128)} copy(f32[2,1,512,512]{3,2,1,0:T(8,128)S(1)} %get-tuple-element.2) | data formatting | bytes 4194304
  78.8 0.8 copy.10

commit v4 on v3

--- a/solution.py
+++ b/solution.py
@@ -169,15 +169,10 @@
 
     barrier = pltpu.get_barrier_semaphore()
 
-    def greet(k, carry):
-        @pl.when(k > 0)
-        def _():
+    for k in range(pairs):
+        if k > 0:
             pl.semaphore_signal(barrier, inc=1, device_id=same_half(k), device_id_type=MESH)
-
         pl.semaphore_signal(barrier, inc=1, device_id=other_half(k), device_id_type=MESH)
-        return carry
-
-    lax.fori_loop(0, pairs, greet, 0)
 
     def stage_gradients(step):
         def one(slot, carry):
@@ -340,11 +335,26 @@
                 mirrored, turned[rest, :], facts[which, rest, :].astype(jnp.float32)
             )
 
-    for step in range(1, steps):
+    for step in range(1, steps - 1):
         wait_gradients(step)
         add_gram(step)
-
+    scale_back = 1.0 / side
+    for which in range(2):
+        nf_ref[which, 0] += acc[which] * scale_back
     hs = side // 2
+    wait_gradients(steps - 1)
+    last = grads[steps - 1]
+    grams = (
+        (
+            dot(last[:hs], last, ((1,), (1,))),
+            dot(last[hs:], last[hs:], ((1,), (1,))),
+        ),
+        (
+            dot(last[:, :hs], last, ((0,), (0,))),
+            dot(last[:, hs:], last[:, hs:], ((0,), (0,))),
+        ),
+    )
+
 
     def unit_of(shape):
         hit = lax.broadcasted_iota(jnp.int32, shape, 0) == lax.broadcasted_iota(jnp.int32, shape, 1)
@@ -369,12 +379,18 @@
     sides = range(2)
     m, x = [], []
     for which in sides:
-        stat = nf_ref[which, 0] + acc[which] / side
-        nf_ref[which, 0] = stat
-        total = jnp.sum(jnp.sum(stat * stat, axis=0, keepdims=True), axis=1, keepdims=True)
+        upper = nf_ref[which, 0, pl.ds(0, hs), :] + grams[which][0] * scale_back
+        corner = nf_ref[which, 0, pl.ds(hs, hs), pl.ds(hs, hs)] + grams[which][1] * scale_back
+        nf_ref[which, 0, pl.ds(0, hs), :] = upper
+        nf_ref[which, 0, pl.ds(hs, hs), pl.ds(0, hs)] = upper[:, hs:].T
+        nf_ref[which, 0, pl.ds(hs, hs), pl.ds(hs, hs)] = corner
+        across = upper[:, hs:]
+        squares = upper[:, :hs] * upper[:, :hs] + 2.0 * (across * across) + corner * corner
+        total = jnp.sum(jnp.sum(squares, axis=0, keepdims=True), axis=1, keepdims=True)
         frobenius = jnp.sqrt(total)
         start = 1.0 / jnp.sqrt(jnp.sqrt(frobenius))
-        scaled = (stat[:hs] / frobenius, stat[hs:, hs:] / frobenius)
+        shrink = 1.0 / frobenius
+        scaled = (upper * shrink, corner * shrink)
         m.append(scaled)
         x.append(per_part(lambda u, v: start * (1.25 * u - 0.25 * v), unit, scaled))
 
@@ -463,7 +479,7 @@
         upd_ref[block] = returned[inverse_ref[block]]
         return carry
 
-    lax.fori_loop(0, blocks, unpack, 0)
+    lax.fori_loop(0, blocks, unpack, 0, unroll=8)
     pltpu.make_async_copy(
         moved.at[pl.ds(0, most), :], moved.at[pl.ds(0, most), :], u_send
     ).wait()

time: 79.8 us -> 78.9 us (0.989)
  Pallas kernels: 76.8 us -> 76 us
    pallas_call x1, Pallas kernels: 76.8 us -> 76 us  [fused_body(): pl.pallas_call(functools.partial(fused_kernel, rows_of, cols_of), out_sha...]
where the time goes in v4:
time: 78.9 us; the launch traced here: 78.7 us
  Pallas kernels  76 us (96%)
  local copies, waits for them, and re-layouts  2.11 us (3%)
    pallas_call x1, Pallas kernels, fused_body(): pl.pallas_call(functools.partial(fused_kernel, rows_of, cols_of), out_sha...  76 us
    unnamed x2, local copies, waits for them, and re-layouts  2.11 us

profile of v4, /device:TPU:0, one launch (start us, length us, event | category | flops | bytes accessed | tf_op | source)
XLA Modules:
  0.0 78.7 jit_solution(12771075348395193242)
XLA Ops:
  0.6 76.0 %shard_map.68 = (f32[2,1,512,512]{3,2,1,0:T(8,128)S(1)}, bf16[32,16,512]{2,1,0:T(8,128)(2,1)S(1)}) custom-call(s32[32]{0:T(128)} %slot_ref.1, s32[32]{0:T(128)} %layer_ref.1, f32[4]{0:T(128)} %scale_ref.1, bf16[3,32,16,512]{3,2,1,0:T(8,128)(2,1)} %g_far.1, f32[2,32,16,512]{3,2,1,0:T(8,128)} %f_far.1), custom_call_target="tpu_custom_call" | custom-call | tf_op jit(solution)/shard_map/pallas_call | solution.py:493
  76.6 1.3 %copy.9 = f32[2,1,512,512]{3,2,1,0:T(8,128)} copy(f32[2,1,512,512]{3,2,1,0:T(8,128)S(1)} %get-tuple-element.2) | data formatting | bytes 4194304
  77.9 0.8 %copy.10 = bf16[32,16,512]{2,1,0:T(8,128)(2,1)} copy(bf16[32,16,512]{2,1,0:T(8,128)(2,1)S(1)} %get-tuple-element.3) | data formatting | bytes 1048576
